TPU v7x, 32 devices: a whole 2x2x4 slice. The times are simulated.
32 devices in a mesh: near: 4 (over x, core), off: 8 (over z, y).
Axes of the slice: x: 2, y: 2, z: 4, core: 2. Of those that a mesh axis runs over, the one named last changes fastest.
Arguments:
- adjoint: float32 [64, 128, 6, 128], P('near', 'off'), may hold values from -6 to 6
- jacobian: bfloat16 [64, 128, 7, 36, 128], P('near', 'off'), may hold values from -1 to 1
- source: float32 [64, 128, 6, 128], P('near', 'off'), may hold values from -4 to 4
- pseudo_step: float32 [64, 128, 128], P('near', 'off'), may hold values from 0.05 to 0.5
- receptor_count: int32 [32], P(('near', 'off')), may hold values from 512 to 1024, as said below
- receptor_cell: int32 [32768], P(('near', 'off')), may hold values from 0 to 32767
- donor_owner: int32 [32768, 1], P(('near', 'off')), may hold values from 0 to 31; in each aligned block of 1024 rows (0 to 1023, 1024 to 2047, ...) at most 48 rows name the same one
- donor_base: int32 [32768], P(('near', 'off')), may hold values from 0 to 30590, as said below
- donor_fraction: float32 [32768, 3], P(('near', 'off')), may hold values from 0 to 1
Outputs:
- residual: float32 [64, 128, 6, 128], P('near', 'off')
- updated: float32 [64, 128, 6, 128], P('near', 'off')
Inputs may be any that keep to these rules, and one draw needn't show every extreme that they name: `receptor_count`: A multiple of 128; rows of a block at or above its count are padding. `donor_owner`: among the 1024 rows of one block, padding included, at most 48 name the same owner block. `donor_base`: the donor cube lies inside the owner block: its lowest corner has ix < 15, iy < 15, iz < 127.
All inputs are finite; a program needn't handle non-finite values.
Results may differ from a plain program's by a relative error of at most 0.0025.
Values may be sent and summed in bfloat16 or wider, within the bound.
A program may use at most 192 MiB of HBM per device.

v0:
```python
import jax
import jax.numpy as jnp
from jax import lax
from jax.sharding import PartitionSpec as P


def passed_along(block, axis, distance):
    devices = range(lax.axis_size(axis))
    route = [(i - distance, i) for i in devices if i - distance in devices]
    return lax.ppermute(block, axis, route)


def moved_z(field, offset):
    length = field.shape[3]
    if offset > 0:
        return lax.slice_in_dim(jnp.pad(field, ((0, 0), (0, 0), (0, 0), (1, 0))), 0, length, axis=3)
    return lax.slice_in_dim(jnp.pad(field, ((0, 0), (0, 0), (0, 0), (0, 1))), 1, length + 1, axis=3)


def transposed(blocks, values):
    matrix = blocks.reshape(
        values.shape[0], values.shape[1], values.shape[2], values.shape[2], values.shape[3]
    )
    return jnp.einsum("xyabz,xyaz->xybz", matrix, values, preferred_element_type=jnp.float32)


def two_point(index, fraction, length):
    positions = jnp.arange(length, dtype=jnp.int32)[None, :]
    lower = jnp.where(positions == index[:, None], 1.0 - fraction[:, None], 0.0)
    upper = jnp.where(positions == index[:, None] + 1, fraction[:, None], 0.0)
    return lower + upper


def shards(
    adjoint,
    jacobian,
    source,
    pseudo_step,
    receptor_count,
    receptor_cell,
    donor_owner,
    donor_base,
    donor_fraction,
):
    size_x = adjoint.shape[0]
    size_y = adjoint.shape[1]
    var_count = adjoint.shape[2]
    size_z = adjoint.shape[3]
    adjoint_low = adjoint.astype(jnp.bfloat16)
    products = [transposed(jacobian[:, :, stencil], adjoint_low) for stencil in range(7)]
    rim_adj, rim_jac = passed_along((adjoint_low[-1:], jacobian[-1:, :, 1]), "near", 1)
    from_low_x = transposed(rim_jac, rim_adj)
    rim_adj, rim_jac = passed_along((adjoint_low[:1], jacobian[:1, :, 2]), "near", -1)
    from_high_x = transposed(rim_jac, rim_adj)
    rim_adj, rim_jac = passed_along((adjoint_low[:, -1:], jacobian[:, -1:, 3]), "off", 1)
    from_low_y = transposed(rim_jac, rim_adj)
    rim_adj, rim_jac = passed_along((adjoint_low[:, :1], jacobian[:, :1, 4]), "off", -1)
    from_high_y = transposed(rim_jac, rim_adj)
    flux = products[0]
    flux = flux + jnp.concatenate([from_low_x, products[1][: size_x - 1]], axis=0)
    flux = flux + jnp.concatenate([products[2][1:], from_high_x], axis=0)
    flux = flux + jnp.concatenate([from_low_y, products[3][:, : size_y - 1]], axis=1)
    flux = flux + jnp.concatenate([products[4][:, 1:], from_high_y], axis=1)
    flux = flux + moved_z(products[5], 1) + moved_z(products[6], -1)
    near_count = lax.axis_size("near")
    off_count = lax.axis_size("off")
    block_count = near_count * off_count
    row_count = receptor_cell.shape[0]
    capacity = max(2, 3 * row_count // (2 * block_count))
    live = jnp.arange(row_count, dtype=jnp.int32) < receptor_count[0]
    cell_x = receptor_cell // (size_y * size_z)
    cell_y = receptor_cell // size_z % size_y
    cell_z = receptor_cell % size_z
    adjoint_rows = adjoint_low[cell_x, cell_y, :, cell_z].astype(jnp.float32)
    payload = jnp.concatenate([adjoint_rows, donor_fraction], axis=1)
    width = payload.shape[1]
    owner = donor_owner[:, 0]
    matches = (owner[:, None] == jnp.arange(block_count, dtype=jnp.int32)[None, :]) & live[:, None]
    ranks = jnp.cumsum(matches.astype(jnp.int32), axis=0) - 1
    slot_index = jnp.sum(jnp.where(matches, ranks, 0), axis=1)
    target = jnp.where(live, owner, block_count)
    outgoing = (
        jnp.zeros((block_count, capacity, width), jnp.float32)
        .at[target, slot_index]
        .set(payload, mode="drop")
    )
    out_base = (
        jnp.zeros((block_count, capacity), jnp.int32)
        .at[target, slot_index]
        .set(donor_base, mode="drop")
    )
    received_values, received_base = (
        lax.all_to_all(outgoing, ("near", "off"), split_axis=0, concat_axis=0, tiled=True),
        lax.all_to_all(out_base, ("near", "off"), split_axis=0, concat_axis=0, tiled=True),
    )
    incoming = received_values.reshape(block_count * capacity, width)
    arrived = received_base.reshape(block_count * capacity)
    adjoint_in = incoming[:, :var_count]
    fraction = incoming[:, var_count : var_count + 3]
    donor_x = arrived // (size_y * size_z)
    donor_y = arrived // size_z % size_y
    donor_z = arrived % size_z
    weight_x = two_point(donor_x, fraction[:, 0], size_x)
    weight_y = two_point(donor_y, fraction[:, 1], size_y)
    weight_z = two_point(donor_z, fraction[:, 2], size_z)
    spread = -weight_x[:, :, None, None] * weight_y[:, None, :, None] * adjoint_in[:, None, None, :]
    overset = jnp.einsum("rxyv,rz->xyvz", spread, weight_z, precision=lax.Precision.HIGHEST)
    residual = flux + overset + source
    updated = adjoint - pseudo_step[:, :, None, :] * residual
    return (residual, updated)


def solution(mesh):
    in_specs = (
        P("near", "off", None, None),
        P("near", "off", None, None, None),
        P("near", "off", None, None),
        P("near", "off", None),
        P(("near", "off")),
        P(("near", "off")),
        P(("near", "off"), None),
        P(("near", "off")),
        P(("near", "off"), None),
    )
    out_specs = (P("near", "off", None, None), P("near", "off", None, None))
    return jax.shard_map(shards, mesh=mesh, in_specs=in_specs, out_specs=out_specs, check_vma=False)
```

profile of v0, /device:TPU:10, one launch (start us, length us, event | category | flops | bytes accessed | tf_op | source)
XLA Modules:
  0.0 197.4 jit_solution(8024029570080969984)
XLA Ops:
  2.0 9.0 %reduce-window.6 = s32[32,8,128]{2,1,0:T(8,128)S(1)} reduce-window(s32[32,8,128]{2,1,0:T(8,128)S(1)} %fusion.33, s32[]{:T(128)} %constant.89.clone.1), window={size=1x1x128 pad=0_0x0_0x127_0}, to_apply=%region_0.1 | reduce-window | flops 4161536 | bytes 262148 | tf_op jit(solution)/shard_map/reduce-window
  14.4 4.5 %scatter_custom_fusion = s32[1536]{0:T(1024)S(1)} fusion(s32[1024]{0:T(1024)S(1)} %broadcast_select_fusion, s32[1024]{0:T(1024)} %param.16, s32[]{:T(128)} %constant.89.clone.1), kind=kCustom, calls=%fused_computation.121 | custom fusion | bytes 6656
  19.6 6.0 %all-to-all-start = ((s32[32,1,48]{2,1,0:T(1,128)}), s32[32,1,48]{2,1,0:T(1,128)S(1)}, u32[]{:S(2)}, u32[]{:S(2)}) async-start(s32[32,1,48]{2,1,0:T(1,128)} %all_to_all.9), calls=%async_computation | async-start | bytes 32768 | tf_op jit(solution)/shard_map/all_to_all | solution.py:94
  27.3 2.2 %collective-permute-start.3 = (bf16[1,16,36,128]{3,1,2,0:T(8,128)(2,1)}, bf16[1,16,36,128]{3,1,2,0:T(8,128)(2,1)}, u32[]{:S(2)}, u32[]{:S(2)}) collective-permute-start(bf16[1,16,36,128]{3,1,2,0:T(8,128)(2,1)} %get-tuple-element.19), channel_id=1, source_target_pairs={{8,0},{16,8},{24,16},{9,1},{17,9},{25,17},{10,2},{18,10},{26,18},{... | collective-permute-start | bytes 442376 | tf_op jit(solution)/shard_map/ppermute | solution.py:10
  29.6 2.7 %collective-permute-start.1 = (bf16[1,16,36,128]{3,1,2,0:T(8,128)(2,1)}, bf16[1,16,36,128]{3,1,2,0:T(8,128)(2,1)}, u32[]{:S(2)}, u32[]{:S(2)}) collective-permute-start(bf16[1,16,36,128]{3,1,2,0:T(8,128)(2,1)} %get-tuple-element.20), channel_id=1, source_target_pairs={{0,8},{8,16},{16,24},{1,9},{9,17},{17,25},{2,10},{10,18},{18,26},{... | collective-permute-start | bytes 442376 | tf_op jit(solution)/shard_map/ppermute | solution.py:10
  35.1 3.4 %collective-permute-start.5 = (bf16[16,1,36,128]{3,0,2,1:T(8,128)(2,1)}, bf16[16,1,36,128]{3,0,2,1:T(8,128)(2,1)}, u32[]{:S(2)}, u32[]{:S(2)}) collective-permute-start(bf16[16,1,36,128]{3,0,2,1:T(8,128)(2,1)} %bitcast.119), channel_id=1, source_target_pairs={{0,1},{1,2},{2,3},{3,4},{4,5},{5,6},{6,7},{8,9},{9,10},{10,11},{11... | collective-permute-start | bytes 442376 | tf_op jit(solution)/shard_map/ppermute | solution.py:10
  39.1 3.4 %collective-permute-start.7 = (bf16[16,1,36,128]{3,0,2,1:T(8,128)(2,1)}, bf16[16,1,36,128]{3,0,2,1:T(8,128)(2,1)}, u32[]{:S(2)}, u32[]{:S(2)}) collective-permute-start(bf16[16,1,36,128]{3,0,2,1:T(8,128)(2,1)} %bitcast.118), channel_id=1, source_target_pairs={{1,0},{2,1},{3,2},{4,3},{5,4},{6,5},{7,6},{9,8},{10,9},{11,10},{12... | collective-permute-start | bytes 442376 | tf_op jit(solution)/shard_map/ppermute | solution.py:10
  42.5 7.6 %copy.44 = bf16[16,16,6,128]{2,3,1,0:T(8,128)(2,1)} copy(f32[16,16,6,128]{3,1,2,0:T(8,128)} %param.9) | data formatting | bytes 1179648 | tf_op args[0]
  50.1 2.3 %fusion.55 = (bf16[16,1,6,128]{2,3,1,0:T(8,128)(2,1)}, bf16[16,1,6,128]{2,3,1,0:T(8,128)(2,1)}) fusion(bf16[16,16,6,128]{2,3,1,0:T(8,128)(2,1)} %copy.44), kind=kLoop, calls=%fused_computation.138 | loop fusion | bytes 98304 | tf_op jit(solution)/shard_map/slice | solution.py:57
  52.4 3.1 %collective-permute-start.6 = (bf16[16,1,6,128]{2,3,1,0:T(8,128)(2,1)}, bf16[16,1,6,128]{2,3,1,0:T(8,128)(2,1)}, u32[]{:S(2)}, u32[]{:S(2)}) collective-permute-start(bf16[16,1,6,128]{2,3,1,0:T(8,128)(2,1)} %get-tuple-element.28), channel_id=1, source_target_pairs={{1,0},{2,1},{3,2},{4,3},{5,4},{6,5},{7,6},{9,8},{10,9},{11,10},{12... | collective-permute-start | bytes 73736 | tf_op jit(solution)/shard_map/ppermute | solution.py:10
  55.5 2.3 %fusion.56 = (bf16[1,16,6,128]{2,3,1,0:T(8,128)(2,1)}, bf16[1,16,6,128]{2,3,1,0:T(8,128)(2,1)}) fusion(bf16[16,16,6,128]{2,3,1,0:T(8,128)(2,1)} %copy.44), kind=kLoop, calls=%fused_computation.139 | loop fusion | bytes 98304 | tf_op jit(solution)/shard_map/slice | solution.py:53
  57.8 11.2 %bitcast_convert_fusion = f32[16,16,128,6]{3,2,1,0:T(8,128)} fusion(bf16[16,16,6,128]{2,3,1,0:T(8,128)(2,1)} %copy.44), kind=kLoop, calls=%fused_computation.5 | loop fusion | flops 196608 | bytes 1179648
  69.0 11.8 %fusion.54 = (bf16[16,16,1,36,128]{4,1,3,2,0:T(8,128)(2,1)S(1)}, bf16[16,16,1,36,128]{4,1,3,2,0:T(8,128)(2,1)}, bf16[16,16,1,36,128]{4,1,3,2,0:T(8,128)(2,1)}, b...) fusion(bf16[16,16,7,36,128]{4,1,3,2,0:T(8,128)(2,1)} %param.10), kind=kLoop, calls=%fused_computation.137 | loop fusion | bytes 33030144 | tf_op jit(solution)/shard_map/slice | solution.py:50
  81.9 13.7 %gather_fusion = bf16[1024,6]{1,0:T(8,128)(2,1)S(1)} fusion(bf16[16,16,6,128]{2,3,1,0:T(8,128)(2,1)} %copy.44, s32[1024]{0:T(1024)S(1)} %fusion.43), kind=kCustom, calls=%fused_computation | custom fusion | bytes 36864 | tf_op jit(solution)/shard_map/gather | solution.py:74
  96.4 4.2 %scatter_custom_fusion.1 = f32[9,1536]{0,1:T(8,128)S(1)} fusion(s32[1024]{0:T(1024)S(1)} %broadcast_select_fusion, f32[1024,3]{1,0:T(8,128)} %copy.51, f32[]{:T(128)} %constant.160, f32[1024,6]{1,0:T(8,128)} %convert_element_type.17, f32[]{:T(128)} %constant.88.clone.1), kind=kCustom, calls=%fused_computation.33 | custom fusion | flops 9216 | bytes 92168
  100.9 10.0 %copy.134 = f32[16,16,128,6]{2,1,3,0:T(8,128)S(1)} copy(f32[16,16,128,6]{3,2,1,0:T(8,128)} %bitcast_convert_fusion) | data formatting | bytes 1572864
  110.9 10.2 %multiply_reduce_fusion.6 = (f32[16,16,128,6]{2,1,3,0:T(8,128)}, f32[16,16,128,6]{2,1,3,0:T(8,128)}, f32[16,16,128,6]{2,1,3,0:T(8,128)}, f32[16,16,128,6]{2,1,3,...) fusion(bf16[16,16,128,6,6]{2,1,4,3,0:T(8,128)(2,1)} %bitcast.131, ...), kind=kLoop, calls=%fused_computation.12 | loop fusion | flops 23396352 | bytes 22806528 | tf_op jit(solution)/shard_map/xyabz,xyaz->xybz/dot_general | solution.py:24
  128.2 5.9 %all-to-all-start.1 = ((f32[32,1,432]{2,1,0:T(1,128)}), f32[32,1,432]{2,1,0:T(1,128)S(1)}, u32[]{:S(2)}, u32[]{:S(2)}) async-start(f32[32,1,432]{2,1,0:T(1,128)} %reshape.466), calls=%async_computation.1 | async-start | bytes 131072 | tf_op jit(solution)/shard_map/all_to_all | solution.py:93
  136.1 3.4 %collective-permute-start.4 = (bf16[16,1,6,128]{2,3,1,0:T(8,128)(2,1)S(1)}, bf16[16,1,6,128]{2,3,1,0:T(8,128)(2,1)S(1)}, u32[]{:S(2)}, u32[]{:S(2)}) collective-permute-start(bf16[16,1,6,128]{2,3,1,0:T(8,128)(2,1)S(1)} %copy-done.5), channel_id=1, source_target_pairs={{0,1},{1,2},{2,3},{3,4},{4,5},{5,6},{6,7},{8,9},{9,10},{10,11},{11... | collective-permute-start | bytes 73736 | tf_op jit(solution)/shard_map/ppermute | solution.py:10
  140.7 12.2 %collective-permute-done.4 = bf16[16,1,6,128]{2,3,1,0:T(8,128)(2,1)S(1)} collective-permute-done((bf16[16,1,6,128]{2,3,1,0:T(8,128)(2,1)S(1)}, bf16[16,1,6,128]{2,3,1,0:T(8,128)(2,1)S(1)}, u32[]{:S(2)}, u32[]{:S(2)}) %collective-permute-start.4) | collective-permute-done | bytes 24608 | tf_op jit(solution)/shard_map/ppermute | solution.py:10
  154.9 6.6 %collective-permute-done.2 = bf16[1,16,6,128]{2,3,1,0:T(8,128)(2,1)S(1)} collective-permute-done((bf16[1,16,6,128]{2,3,1,0:T(8,128)(2,1)S(1)}, bf16[1,16,6,128]{2,3,1,0:T(8,128)(2,1)S(1)}, u32[]{:S(2)}, u32[]{:S(2)}) %collective-permute-start.2) | collective-permute-done | bytes 24608 | tf_op jit(solution)/shard_map/ppermute | solution.py:10
  163.5 8.8 %collective-permute-done = bf16[1,16,6,128]{2,3,1,0:T(8,128)(2,1)S(1)} collective-permute-done((bf16[1,16,6,128]{2,3,1,0:T(8,128)(2,1)}, bf16[1,16,6,128]{2,3,1,0:T(8,128)(2,1)S(1)}, u32[]{:S(2)}, u32[]{:S(2)}) %collective-permute-start) | collective-permute-done | bytes 24608 | tf_op jit(solution)/shard_map/ppermute | solution.py:10
  176.3 2.3 %copy.135 = f32[16,128,6]{1,0,2:T(8,128)} copy(f32[16,128,6]{2,1,0:T(8,128)} %bitcast_convert_fusion.4) | data formatting | bytes 98304
  186.1 11.3 %multiply_subtract_fusion = (f32[16,16,6,128]{3,1,2,0:T(8,128)}, f32[16,16,6,128]{3,1,2,0:T(8,128)}) fusion(f32[16,16,6,128]{3,1,2,0:T(8,128)} %param.9, f32[16,16,128]{2,1,0:T(8,128)} %param.12, f32[16,16,6,128]{3,1,2,0:T(8,128)} %param.11, f32[1536]{0:T(1024)S(1)} %get-tuple-element.12, s32[1536]{0:T(1024)} %get-tuple-element.33, ...), kind=kOutput, calls=%fused_computation.26 | convolution fusion | flops 3629973504 | bytes 10416128 | tf_op jit(solution)/shard_map/rxyv,rz->xyvz/dot_general | solution.py:107
  (79 shorter events, 37.7 us)
Async XLA Ops:
  19.6 108.6 %all-to-all-start = ((s32[32,1,48]{2,1,0:T(1,128)}), s32[32,1,48]{2,1,0:T(1,128)S(1)}, u32[]{:S(2)}, u32[]{:S(2)}) async-start(s32[32,1,48]{2,1,0:T(1,128)} %all_to_all.9), calls=%async_computation | async-start | bytes 32768 | tf_op jit(solution)/shard_map/all_to_all | solution.py:94
  27.3 156.8 %collective-permute-start.3 = (bf16[1,16,36,128]{3,1,2,0:T(8,128)(2,1)}, bf16[1,16,36,128]{3,1,2,0:T(8,128)(2,1)}, u32[]{:S(2)}, u32[]{:S(2)}) collective-permute-start(bf16[1,16,36,128]{3,1,2,0:T(8,128)(2,1)} %get-tuple-element.19), channel_id=1, source_target_pairs={{8,0},{16,8},{24,16},{9,1},{17,9},{25,17},{10,2},{18,10},{26,18},{... | collective-permute-start | bytes 442376 | tf_op jit(solution)/shard_map/ppermute | solution.py:10
  29.6 155.6 %collective-permute-start.1 = (bf16[1,16,36,128]{3,1,2,0:T(8,128)(2,1)}, bf16[1,16,36,128]{3,1,2,0:T(8,128)(2,1)}, u32[]{:S(2)}, u32[]{:S(2)}) collective-permute-start(bf16[1,16,36,128]{3,1,2,0:T(8,128)(2,1)} %get-tuple-element.20), channel_id=1, source_target_pairs={{0,8},{8,16},{16,24},{1,9},{9,17},{17,25},{2,10},{10,18},{18,26},{... | collective-permute-start | bytes 442376 | tf_op jit(solution)/shard_map/ppermute | solution.py:10
  35.1 148.0 %collective-permute-start.5 = (bf16[16,1,36,128]{3,0,2,1:T(8,128)(2,1)}, bf16[16,1,36,128]{3,0,2,1:T(8,128)(2,1)}, u32[]{:S(2)}, u32[]{:S(2)}) collective-permute-start(bf16[16,1,36,128]{3,0,2,1:T(8,128)(2,1)} %bitcast.119), channel_id=1, source_target_pairs={{0,1},{1,2},{2,3},{3,4},{4,5},{5,6},{6,7},{8,9},{9,10},{10,11},{11... | collective-permute-start | bytes 442376 | tf_op jit(solution)/shard_map/ppermute | solution.py:10
  39.1 143.0 %collective-permute-start.7 = (bf16[16,1,36,128]{3,0,2,1:T(8,128)(2,1)}, bf16[16,1,36,128]{3,0,2,1:T(8,128)(2,1)}, u32[]{:S(2)}, u32[]{:S(2)}) collective-permute-start(bf16[16,1,36,128]{3,0,2,1:T(8,128)(2,1)} %bitcast.118), channel_id=1, source_target_pairs={{1,0},{2,1},{3,2},{4,3},{5,4},{6,5},{7,6},{9,8},{10,9},{11,10},{12... | collective-permute-start | bytes 442376 | tf_op jit(solution)/shard_map/ppermute | solution.py:10
  52.4 83.7 %collective-permute-start.6 = (bf16[16,1,6,128]{2,3,1,0:T(8,128)(2,1)}, bf16[16,1,6,128]{2,3,1,0:T(8,128)(2,1)}, u32[]{:S(2)}, u32[]{:S(2)}) collective-permute-start(bf16[16,1,6,128]{2,3,1,0:T(8,128)(2,1)} %get-tuple-element.28), channel_id=1, source_target_pairs={{1,0},{2,1},{3,2},{4,3},{5,4},{6,5},{7,6},{9,8},{10,9},{11,10},{12... | collective-permute-start | bytes 73736 | tf_op jit(solution)/shard_map/ppermute | solution.py:10
  69.0 11.8 %copy-start.7 = (s32[1024]{0:T(1024)S(1)}, s32[1024]{0:T(1024)}, u32[]{:S(2)}) copy-start(s32[1024]{0:T(1024)} %param.14) | copy-start | bytes 12292
  69.0 11.8 %copy-start.6 = (f32[1024,3]{0,1:T(4,128)S(1)}, f32[1024,3]{0,1:T(4,128)}, u32[]{:S(2)}) copy-start(f32[1024,3]{0,1:T(4,128)} %param.17) | copy-start | bytes 36868
  121.2 15.0 %copy-start.5 = (bf16[16,1,6,128]{2,3,1,0:T(8,128)(2,1)S(1)}, bf16[16,1,6,128]{2,3,1,0:T(8,128)(2,1)}, u32[]{:S(2)}) copy-start(bf16[16,1,6,128]{2,3,1,0:T(8,128)(2,1)} %get-tuple-element.29) | copy-start | bytes 73732
  121.2 31.7 %copy-start.4 = (bf16[1,16,6,128]{2,3,1,0:T(8,128)(2,1)S(1)}, bf16[1,16,6,128]{2,3,1,0:T(8,128)(2,1)}, u32[]{:S(2)}) copy-start(bf16[1,16,6,128]{2,3,1,0:T(8,128)(2,1)} %get-tuple-element.30) | copy-start | bytes 73732
  128.2 50.4 %all-to-all-start.1 = ((f32[32,1,432]{2,1,0:T(1,128)}), f32[32,1,432]{2,1,0:T(1,128)S(1)}, u32[]{:S(2)}, u32[]{:S(2)}) async-start(f32[32,1,432]{2,1,0:T(1,128)} %reshape.466), calls=%async_computation.1 | async-start | bytes 131072 | tf_op jit(solution)/shard_map/all_to_all | solution.py:93
  136.1 16.8 %collective-permute-start.4 = (bf16[16,1,6,128]{2,3,1,0:T(8,128)(2,1)S(1)}, bf16[16,1,6,128]{2,3,1,0:T(8,128)(2,1)S(1)}, u32[]{:S(2)}, u32[]{:S(2)}) collective-permute-start(bf16[16,1,6,128]{2,3,1,0:T(8,128)(2,1)S(1)} %copy-done.5), channel_id=1, source_target_pairs={{0,1},{1,2},{2,3},{3,4},{4,5},{5,6},{6,7},{8,9},{9,10},{10,11},{11... | collective-permute-start | bytes 73736 | tf_op jit(solution)/shard_map/ppermute | solution.py:10
  152.9 8.6 %collective-permute-start.2 = (bf16[1,16,6,128]{2,3,1,0:T(8,128)(2,1)S(1)}, bf16[1,16,6,128]{2,3,1,0:T(8,128)(2,1)S(1)}, u32[]{:S(2)}, u32[]{:S(2)}) collective-permute-start(bf16[1,16,6,128]{2,3,1,0:T(8,128)(2,1)S(1)} %copy-done.4), channel_id=1, source_target_pairs={{8,0},{16,8},{24,16},{9,1},{17,9},{25,17},{10,2},{18,10},{26,18},{... | collective-permute-start | bytes 73736 | tf_op jit(solution)/shard_map/ppermute | solution.py:10
  161.5 10.9 %collective-permute-start = (bf16[1,16,6,128]{2,3,1,0:T(8,128)(2,1)}, bf16[1,16,6,128]{2,3,1,0:T(8,128)(2,1)S(1)}, u32[]{:S(2)}, u32[]{:S(2)}) collective-permute-start(bf16[1,16,6,128]{2,3,1,0:T(8,128)(2,1)} %get-tuple-element.31), channel_id=1, source_target_pairs={{0,8},{8,16},{16,24},{1,9},{9,17},{17,25},{2,10},{10,18},{18,26},{... | collective-permute-start | bytes 73736 | tf_op jit(solution)/shard_map/ppermute | solution.py:10
  174.4 11.7 %copy-start = (f32[16,16,128,6]{2,1,3,0:T(8,128)S(1)}, f32[16,16,128,6]{2,1,3,0:T(8,128)}, u32[]{:S(2)}) copy-start(f32[16,16,128,6]{2,1,3,0:T(8,128)} %get-tuple-element.2) | copy-start | bytes 2359300
  175.4 10.7 %copy-start.1 = (f32[16,16,128,6]{2,1,3,0:T(8,128)S(1)}, f32[16,16,128,6]{2,1,3,0:T(8,128)}, u32[]{:S(2)}) copy-start(f32[16,16,128,6]{2,1,3,0:T(8,128)} %get-tuple-element.5) | copy-start | bytes 2359300
  176.3 9.8 %copy-start.2 = (f32[16,16,128,6]{2,1,3,0:T(8,128)S(1)}, f32[16,16,128,6]{2,1,3,0:T(8,128)}, u32[]{:S(2)}) copy-start(f32[16,16,128,6]{2,1,3,0:T(8,128)} %get-tuple-element.7) | copy-start | bytes 2359300
  176.3 9.8 %copy-start.3 = (f32[16,16,128,6]{2,1,3,0:T(8,128)S(1)}, f32[16,16,128,6]{2,1,3,0:T(8,128)}, u32[]{:S(2)}) copy-start(f32[16,16,128,6]{2,1,3,0:T(8,128)} %get-tuple-element.8) | copy-start | bytes 2359300
where the time goes:
time: 199 us; the launch traced here: 197 us
  local copies, waits for them, and re-layouts  73.4 us (37%)
  other arithmetic  49.5 us (25%)
  starting transfers between devices  33.9 us (17%)
  waiting for transfers between devices  27.7 us (14%)
  matrix products  11.3 us (6%)
    unnamed x30, local copies, waits for them, and re-layouts  30.9 us
    ppermute x8, waiting for transfers between devices, passed_along(): return lax.ppermute(block, axis, route)  27.7 us
    ppermute x8, starting transfers between devices, passed_along(): return lax.ppermute(block, axis, route)  22 us
    unnamed x9, other arithmetic  19.3 us
    dot_general x5, other arithmetic, transposed(): jnp.einsum('xyabz,xyaz->xybz', matrix, values, preferred_element_type=jnp...  14 us
    gather x1, local copies, waits for them, and re-layouts, shards(): adjoint_rows = adjoint_low[cell_x, cell_y, :, cell_z].astype(jnp.float32)  13.7 us
    slice x1, local copies, waits for them, and re-layouts, shards(): jacobian[:, :, stencil]  11.8 us
    dot_general x1, matrix products, shards(): jnp.einsum('rxyv,rz->xyvz', spread, weight_z, precision=lax.Precision.HIG...  11.3 us
  transfers between devices with their start and end apart: 10, of which 3 were waited for; matrix products, arithmetic and copies ran while one was open for 53% of the time, Pallas kernels for 0%

commit v1 on v0

v1 whole, which is shorter than its diff:
```python
import functools

import jax
import jax.numpy as jnp
from jax import lax
from jax.experimental import pallas as pl
from jax.experimental.pallas import tpu as pltpu
from jax.sharding import PartitionSpec as P

F32 = jnp.float32
BF16 = jnp.bfloat16
VMEM_LIMIT = 58 * 1024 * 1024
NT = (((1,), (1,)), ((), ()))


def fold(product, var_count):
    total = product[..., 0:var_count, :]
    for a in range(1, var_count):
        total = total + product[..., a * var_count : (a + 1) * var_count, :]
    return total


def spread_adjoint(adj_ref, wide_ref):
    size_x, size_y, var_count, size_z = adj_ref.shape
    rows = var_count * var_count
    side = jnp.zeros((size_y + 2, rows, size_z), F32)
    wide_ref[0] = side
    wide_ref[size_x + 1] = side
    edge = jnp.zeros((rows, size_z), F32)

    def plane(x, carry):
        wide_ref[x + 1, 0] = edge
        wide_ref[x + 1, size_y + 1] = edge
        low = adj_ref[x].astype(BF16).astype(F32)
        for a in range(var_count):
            wide_ref[x + 1, 1 : size_y + 1, a * var_count : (a + 1) * var_count, :] = jnp.broadcast_to(
                low[:, a : a + 1, :], (size_y, var_count, size_z)
            )
        return carry

    lax.fori_loop(0, size_x, plane, 0)


def pack_rows(count_ref, cell_ref, owner_ref, base_ref, frac_ref, adj_ref, padded_ref, masked_ref, me, blocks, stride):
    size_x, size_y, var_count, size_z = adj_ref.shape
    rows = cell_ref.shape[1]
    lanes = 128
    z_bits = size_z.bit_length() - 1
    row = lax.broadcasted_iota(jnp.int32, (1, rows), 1)
    live = row < count_ref[0]
    cell = cell_ref[...]
    cell_z = cell & (size_z - 1)
    cell_xy = cell >> z_bits
    hot_z = jnp.where(lax.broadcasted_iota(jnp.int32, (size_z, rows), 0) == cell_z, 1.0, 0.0).astype(BF16)
    padded_ref[:, var_count:8, :] = jnp.zeros((size_y, 8 - var_count, size_z), F32)

    def gather(x, mu):
        padded_ref[:, 0:var_count, :] = adj_ref[x]
        plane = padded_ref[...].reshape(size_y * 8, size_z).astype(BF16)
        picked = jnp.dot(plane, hot_z, preferred_element_type=F32)
        for y in range(size_y):
            mu = jnp.where(cell_xy == x * size_y + y, picked[y * 8 : y * 8 + 8], mu)
        return mu

    mu = lax.fori_loop(0, size_x, gather, jnp.zeros((8, rows), F32))
    base = base_ref[...]
    base_xy = (base >> z_bits).astype(F32)
    base_z = (base & (size_z - 1)).astype(F32)
    sub = lax.broadcasted_iota(jnp.int32, (8, rows), 0)
    top = jnp.where(sub < var_count, mu, jnp.where(sub == var_count, base_xy, base_z))
    frac = frac_ref[...]
    frac_hi = frac.astype(BF16).astype(F32)
    payload = jnp.concatenate([top, frac_hi, frac - frac_hi], axis=0)
    owner = jnp.where(live, owner_ref[...], -1)

    strips = rows // lanes
    block_ids = lax.broadcasted_iota(jnp.int32, (blocks, lanes), 0)
    matches = [
        jnp.where(block_ids == owner[:, s * lanes : (s + 1) * lanes], 1.0, 0.0) for s in range(strips)
    ]
    before = jnp.where(
        lax.broadcasted_iota(jnp.int32, (lanes, lanes), 0) < lax.broadcasted_iota(jnp.int32, (lanes, lanes), 1), 1.0, 0.0
    ).astype(BF16)
    earlier = jnp.dot(jnp.concatenate(matches, axis=0).astype(BF16), before, preferred_element_type=F32)
    carry = jnp.zeros((blocks, 1), F32)
    ranks = []
    for s in range(strips):
        here = earlier[s * blocks : (s + 1) * blocks] + carry
        ranks.append(jnp.sum(here * matches[s], axis=0, keepdims=True))
        carry = carry + jnp.sum(matches[s], axis=1, keepdims=True)
    rank = jnp.concatenate(ranks, axis=1).astype(jnp.int32)
    place = rank + lax.rem(me, lanes // stride) * stride
    hot_rank = jnp.where(lax.broadcasted_iota(jnp.int32, (lanes, rows), 0) == place, 1.0, 0.0).astype(BF16)

    def mask(o, carry):
        masked_ref[pl.ds(pl.multiple_of(o * 16, 16), 16), :] = jnp.where(owner == o, payload, 0.0).astype(BF16)
        return carry

    lax.fori_loop(0, blocks, mask, 0)
    return lax.dot_general(masked_ref[...], hot_rank, NT, preferred_element_type=F32).astype(BF16)


def pack_kernel(blocks, stride, off_count, count_ref, cell_ref, owner_ref, base_ref, frac_ref, adj_ref, jac_ref,
                tiles_ref, rims_ref, wide_ref, rim_ref, padded_ref, masked_ref, sems):
    size_x, size_y, var_count, size_z = adj_ref.shape
    me = lax.axis_index("near") * off_count + lax.axis_index("off")
    sources = (
        jac_ref.at[size_x - 1, :, 1],
        jac_ref.at[0, :, 2],
        jac_ref.at[:, size_y - 1, 3],
        jac_ref.at[:, 0, 4],
    )
    copies = [pltpu.make_async_copy(s, rim_ref.at[i], sems.at[i]) for i, s in enumerate(sources)]
    for copy in copies:
        copy.start()
    spread_adjoint(adj_ref, wide_ref)
    tiles = pack_rows(count_ref, cell_ref, owner_ref, base_ref, frac_ref, adj_ref, padded_ref, masked_ref, me, blocks, stride)
    tiles_ref[...] = tiles.reshape(blocks, 16, 128)
    for copy in copies:
        copy.wait()
    rims_ref[0] = fold(rim_ref[0].astype(F32) * wide_ref[size_x, 1 : size_y + 1], var_count)
    rims_ref[1] = fold(rim_ref[1].astype(F32) * wide_ref[1, 1 : size_y + 1], var_count)
    rims_ref[2] = fold(rim_ref[2].astype(F32) * wide_ref[1 : size_x + 1, size_y], var_count)
    rims_ref[3] = fold(rim_ref[3].astype(F32) * wide_ref[1 : size_x + 1, 1], var_count)


def flux_planes(adj_shape, jac_hbm, jac_ref, wide_ref, flux_ref, sems):
    size_x, size_y, var_count, size_z = adj_shape

    def copy(x):
        return pltpu.make_async_copy(jac_hbm.at[x], jac_ref.at[x], sems.at[x])

    lane = lax.broadcasted_iota(jnp.int32, (var_count, size_z), 1)

    copy(0).wait()

    def plane(x, carry):
        @pl.when(x + 1 < size_x)
        def _():
            copy(x + 1).wait()

        lower = jnp.maximum(x - 1, 0)
        upper = jnp.minimum(x + 1, size_x - 1)

        def column(y, carry):
            left = jnp.maximum(y - 1, 0)
            right = jnp.minimum(y + 1, size_y - 1)
            mine = wide_ref[x + 1, y + 1]
            here = jac_ref[x, y, 0].astype(F32) * mine
            here += jac_ref[lower, y, 1].astype(F32) * wide_ref[x, y + 1]
            here += jac_ref[upper, y, 2].astype(F32) * wide_ref[x + 2, y + 1]
            here += jac_ref[x, left, 3].astype(F32) * wide_ref[x + 1, y]
            here += jac_ref[x, right, 4].astype(F32) * wide_ref[x + 1, y + 2]
            total = fold(here, var_count)
            up = fold(jac_ref[x, y, 5].astype(F32) * mine, var_count)
            down = fold(jac_ref[x, y, 6].astype(F32) * mine, var_count)
            total += jnp.where(lane == 0, 0.0, pltpu.roll(up, 1, 1))
            total += jnp.where(lane == size_z - 1, 0.0, pltpu.roll(down, size_z - 1, 1))
            flux_ref[x, y] = total
            return carry

        lax.fori_loop(0, size_y, column, 0, unroll=4)
        return carry

    lax.fori_loop(0, size_x, plane, 0)


def overset_factors(recv_ref, stride, size_x, size_y, size_z, var_count):
    blocks = recv_ref.shape[0]
    group = 128 // stride
    mus, wxs, wys, wzs = [], [], [], []
    y_bits = size_y.bit_length() - 1

    def hat(index, fraction, length):
        at = lax.broadcasted_iota(jnp.int32, (length, 128), 0)
        return jnp.where(at == index, 1.0 - fraction, jnp.where(at == index + 1, fraction, 0.0))

    for g in range(blocks // group):
        tile = recv_ref[g * group].astype(F32)
        for i in range(1, group):
            tile = tile + recv_ref[g * group + i].astype(F32)
        frac = tile[8:12] + tile[12:16]
        xy = tile[var_count : var_count + 1].astype(jnp.int32)
        z = tile[var_count + 1 : var_count + 2].astype(jnp.int32)
        mus.append(-tile[0:8])
        wxs.append(hat(xy >> y_bits, frac[0:1], size_x))
        wys.append(hat(xy & (size_y - 1), frac[1:2], size_y))
        wzs.append(hat(z, frac[2:3], size_z))
    return tuple(jnp.concatenate(part, axis=1) for part in (mus, wxs, wys, wzs))


def finish_kernel(stride, adj_ref, src_ref, step_ref, recv_ref, rim_xl, rim_xh, rim_yl, rim_yh, jac_hbm,
                  res_ref, upd_ref, jac_ref, wide_ref, wx_ref, wy_ref, wz_ref, left_ref, sems):
    size_x, size_y, var_count, size_z = adj_ref.shape

    def start(x, carry):
        pltpu.make_async_copy(jac_hbm.at[x], jac_ref.at[x], sems.at[x]).start()
        return carry

    lax.fori_loop(0, size_x, start, 0)
    spread_adjoint(adj_ref, wide_ref)
    mu, wx, wy, wz = overset_factors(recv_ref, stride, size_x, size_y, size_z, var_count)
    wx_ref[...] = wx
    wy_ref[...] = wy
    wz_hi = wz.astype(BF16)
    wz_ref[0] = wz_hi
    wz_ref[1] = (wz - wz_hi.astype(F32)).astype(BF16)
    flux_planes(adj_ref.shape, jac_hbm, jac_ref, wide_ref, res_ref, sems)
    res_ref[0] += rim_xl[...]
    res_ref[size_x - 1] += rim_xh[...]
    res_ref[:, 0] += rim_yl[...]
    res_ref[:, size_y - 1] += rim_yh[...]

    def plane(x, carry):
        mux = mu * wx_ref[pl.ds(x, 1), :]
        for y in range(0, size_y, 2):
            pair = jnp.concatenate([mux * wy_ref[y : y + 1, :], mux * wy_ref[y + 1 : y + 2, :]], axis=0)
            left_ref[y * 8 : y * 8 + 16, :] = pair.astype(BF16)
        left = left_ref[...]
        over = lax.dot_general(left, wz_ref[0], NT, preferred_element_type=F32)
        over += lax.dot_general(left, wz_ref[1], NT, preferred_element_type=F32)
        over = over.reshape(size_y, 8, size_z)[:, 0:var_count, :]
        res = res_ref[x] + over + src_ref[x]
        res_ref[x] = res
        upd_ref[x] = adj_ref[x] - step_ref[x][:, None, :] * res
        return carry

    lax.fori_loop(0, size_x, plane, 0)


def passed_along(block, axis, distance):
    devices = range(lax.axis_size(axis))
    route = [(i - distance, i) for i in devices if i - distance in devices]
    return lax.ppermute(block, axis, route)


def shards(adjoint, jacobian, source, pseudo_step, receptor_count, receptor_cell, donor_owner, donor_base, donor_fraction):
    size_x, size_y, var_count, size_z = adjoint.shape
    rows = var_count * var_count
    off_count = lax.axis_size("off")
    blocks = lax.axis_size("near") * off_count
    row_count = receptor_cell.shape[0]
    capacity = max(2, 3 * row_count // (2 * blocks))
    stride = 1 << (capacity - 1).bit_length()
    slots = blocks * stride
    vmem = pl.BlockSpec(memory_space=pltpu.VMEM)
    hbm = pl.BlockSpec(memory_space=pl.ANY)
    frac = jnp.pad(donor_fraction.T, ((0, 1), (0, 0)))
    tiles, rims = pl.pallas_call(
        functools.partial(pack_kernel, blocks, stride, off_count),
        out_shape=(
            jax.ShapeDtypeStruct((blocks, 16, 128), BF16),
            jax.ShapeDtypeStruct((4, size_y, var_count, size_z), F32),
        ),
        in_specs=[pl.BlockSpec(memory_space=pltpu.SMEM)] + [vmem] * 5 + [hbm],
        out_specs=(vmem, vmem),
        scratch_shapes=[
            pltpu.VMEM((size_x + 2, size_y + 2, rows, size_z), F32),
            pltpu.VMEM((4, size_y, rows, size_z), BF16),
            pltpu.VMEM((size_y, 8, size_z), F32),
            pltpu.VMEM((blocks * 16, row_count), BF16),
            pltpu.SemaphoreType.DMA((4,)),
        ],
        compiler_params=pltpu.CompilerParams(vmem_limit_bytes=VMEM_LIMIT),
    )(
        receptor_count,
        receptor_cell.reshape(1, row_count),
        donor_owner.reshape(1, row_count),
        donor_base.reshape(1, row_count),
        frac,
        adjoint,
        jacobian,
    )
    received = lax.all_to_all(tiles, ("near", "off"), split_axis=0, concat_axis=0, tiled=True)
    rim_xl = passed_along(rims[0], "near", 1)
    rim_xh = passed_along(rims[1], "near", -1)
    rim_yl = passed_along(rims[2], "off", 1)
    rim_yh = passed_along(rims[3], "off", -1)
    return tuple(
        pl.pallas_call(
            functools.partial(finish_kernel, stride),
            out_shape=(jax.ShapeDtypeStruct(adjoint.shape, F32), jax.ShapeDtypeStruct(adjoint.shape, F32)),
            in_specs=[vmem] * 8 + [hbm],
            out_specs=(vmem, vmem),
            scratch_shapes=[
                pltpu.VMEM(jacobian.shape, BF16),
                pltpu.VMEM((size_x + 2, size_y + 2, rows, size_z), F32),
                pltpu.VMEM((size_x, slots), F32),
                pltpu.VMEM((size_y, slots), F32),
                pltpu.VMEM((2, size_z, slots), BF16),
                pltpu.VMEM((size_y * 8, slots), BF16),
                pltpu.SemaphoreType.DMA((size_x,)),
            ],
            compiler_params=pltpu.CompilerParams(vmem_limit_bytes=VMEM_LIMIT),
        )(adjoint, source, pseudo_step, received, rim_xl, rim_xh, rim_yl, rim_yh, jacobian)
    )


def solution(mesh):
    in_specs = (
        P("near", "off", None, None),
        P("near", "off", None, None, None),
        P("near", "off", None, None),
        P("near", "off", None),
        P(("near", "off")),
        P(("near", "off")),
        P(("near", "off"), None),
        P(("near", "off")),
        P(("near", "off"), None),
    )
    out_specs = (P("near", "off", None, None), P("near", "off", None, None))
    return jax.shard_map(shards, mesh=mesh, in_specs=in_specs, out_specs=out_specs, check_vma=False)
```

time: 199 us -> 75.7 us (0.38)
  the two profiles are of different devices: /device:TPU:10 before, /device:TPU:6 now
where the time goes in v1:
time: 75.7 us; the launch traced here: 75.2 us
  local copies, waits for them, and re-layouts  27.9 us (37%)
  Pallas kernels  26.8 us (35%)
  starting transfers between devices  17.1 us (23%)
  waiting for transfers between devices  1.91 us (3%)
  between operations  1.4 us (2%)
    unnamed x17, local copies, waits for them, and re-layouts  21.8 us
    pallas_call x1, Pallas kernels, shards(): pl.pallas_call(functools.partial(finish_kernel, stride), out_shape=(jax.S...  19.3 us
    ppermute x4, starting transfers between devices, passed_along(): return lax.ppermute(block, axis, route)  11.1 us
    pallas_call x1, Pallas kernels, shards(): pl.pallas_call(functools.partial(pack_kernel, blocks, stride, off_count),...  7.5 us
    all_to_all x1, starting transfers between devices, shards(): lax.all_to_all(tiles, ('near', 'off'), split_axis=0, concat_axis=0, tiled...  6.08 us
    pallas_call x2, local copies, waits for them, and re-layouts, shards(): pl.pallas_call(functools.partial(finish_kernel, stride), out_shape=(jax.S...  4.49 us
    ppermute x4, waiting for transfers between devices, passed_along(): return lax.ppermute(block, axis, route)  1.9 us
  transfers between devices with their start and end apart: 5, of which 1 were waited for; matrix products, arithmetic and copies ran while one was open for 3% of the time, Pallas kernels for 0%

profile of v1, /device:TPU:6, one launch (start us, length us, event | category | flops | bytes accessed | tf_op | source)
XLA Modules:
  0.0 75.2 jit_solution(12034090844099894400)
XLA Ops:
  1.3 0.0 copy-start.6
  1.3 2.4 %copy.13.adj_ref = f32[16,16,6,128]{3,2,1,0:T(8,128)} copy(f32[16,16,6,128]{3,1,2,0:T(8,128)} %param.9) | data formatting | bytes 1572864 | tf_op args[0]
  3.7 17.0 %copy.12.jac_ref.jac_hbm = bf16[16,16,7,36,128]{4,3,2,1,0:T(8,128)(2,1)} copy(bf16[16,16,7,36,128]{4,1,3,2,0:T(8,128)(2,1)} %param.10) | data formatting | bytes 33030144 | tf_op args[1]
  20.6 0.0 copy-done.6
  20.6 0.6 pad.4.frac_ref
  21.2 7.5 %shard_map.104 = (bf16[32,16,128]{2,1,0:T(8,128)(2,1)}, f32[4,16,6,128]{3,2,1,0:T(8,128)}) custom-call(s32[1]{0:T(128)S(6)} %copy.18.count_ref, s32[1,1024]{1,0:T(1,128)} %bitcast.13, s32[1,1024]{1,0:T(1,128)} %bitcast.14, s32[1,1024]{1,0:T(1,128)} %bitcast.15, f32[4,1024]{1,0:T(4,128)} %pad.4.frac_ref, f32[16,16,6,128]{3,2,1,0:T(8,128)} %copy.13.adj_ref, ...), custom_call_target="tpu_custom_call" | custom-call | tf_op jit(solution)/shard_map/pallas_call | solution.py:249
  28.7 6.1 %all-to-all-start = ((bf16[32,16,128]{2,1,0:T(8,128)(2,1)}), bf16[32,16,128]{2,1,0:T(8,128)(2,1)S(1)}, u32[]{:S(2)}, u32[]{:S(2)}) async-start(bf16[32,16,128]{2,1,0:T(8,128)(2,1)} %get-tuple-element.4), calls=%async_computation | async-start | bytes 262144 | tf_op jit(solution)/shard_map/all_to_all | solution.py:274
  34.8 1.0 %slice_bitcast_fusion = (f32[16,6,128]{2,1,0:T(8,128)S(1)}, f32[16,6,128]{2,1,0:T(8,128)S(1)}, f32[16,6,128]{2,1,0:T(8,128)S(1)}, f32[16,6,128]{2,1,0:T(8,128)S(1)}) fusion(f32[4,16,6,128]{3,2,1,0:T(8,128)} %get-tuple-element.5), kind=kLoop, calls=%fused_computation | loop fusion | bytes 393216 | tf_op jit(solution)/shard_map/squeeze | solution.py:278
  35.8 2.5 %collective-permute-start.3 = (f32[16,6,128]{2,1,0:T(8,128)S(1)}, f32[16,6,128]{2,1,0:T(8,128)S(1)}, u32[]{:S(2)}, u32[]{:S(2)}) collective-permute-start(f32[16,6,128]{2,1,0:T(8,128)S(1)} %get-tuple-element.8), channel_id=1, source_target_pairs={{1,0},{2,1},{3,2},{4,3},{5,4},{6,5},{7,6},{9,8},{10,9},{11,10},{12... | collective-permute-start | bytes 147464 | tf_op jit(solution)/shard_map/ppermute | solution.py:234
  38.3 4.3 %collective-permute-start.2 = (f32[16,6,128]{2,1,0:T(8,128)S(1)}, f32[16,6,128]{2,1,0:T(8,128)S(1)}, u32[]{:S(2)}, u32[]{:S(2)}) collective-permute-start(f32[16,6,128]{2,1,0:T(8,128)S(1)} %get-tuple-element.9), channel_id=1, source_target_pairs={{0,1},{1,2},{2,3},{3,4},{4,5},{5,6},{6,7},{8,9},{9,10},{10,11},{11... | collective-permute-start | bytes 147464 | tf_op jit(solution)/shard_map/ppermute | solution.py:234
  42.6 1.9 %collective-permute-start.1 = (f32[16,6,128]{2,1,0:T(8,128)S(1)}, f32[16,6,128]{2,1,0:T(8,128)S(1)}, u32[]{:S(2)}, u32[]{:S(2)}) collective-permute-start(f32[16,6,128]{2,1,0:T(8,128)S(1)} %get-tuple-element.10), channel_id=1, source_target_pairs={{8,0},{16,8},{24,16},{9,1},{17,9},{25,17},{10,2},{18,10},{26,18},{... | collective-permute-start | bytes 147464 | tf_op jit(solution)/shard_map/ppermute | solution.py:234
  44.5 2.4 %collective-permute-start = (f32[16,6,128]{2,1,0:T(8,128)S(1)}, f32[16,6,128]{2,1,0:T(8,128)S(1)}, u32[]{:S(2)}, u32[]{:S(2)}) collective-permute-start(f32[16,6,128]{2,1,0:T(8,128)S(1)} %get-tuple-element.11), channel_id=1, source_target_pairs={{0,8},{8,16},{16,24},{1,9},{9,17},{17,25},{2,10},{10,18},{18,26},{... | collective-permute-start | bytes 147464 | tf_op jit(solution)/shard_map/ppermute | solution.py:234
  46.9 1.2 %copy.14.src_ref = f32[16,16,6,128]{3,2,1,0:T(8,128)} copy(f32[16,16,6,128]{3,1,2,0:T(8,128)S(1)} %copy-done) | data formatting | bytes 1572864 | tf_op args[2]
  48.1 0.0 collective-permute-done.3.rim_yh
  48.1 0.0 collective-permute-done.2.rim_yl
  48.1 0.0 collective-permute-done.1.rim_xh
  48.2 0.0 copy-start.4
  48.2 1.9 %collective-permute-done.rim_xl = f32[16,6,128]{2,1,0:T(8,128)S(1)} collective-permute-done((f32[16,6,128]{2,1,0:T(8,128)S(1)}, f32[16,6,128]{2,1,0:T(8,128)S(1)}, u32[]{:S(2)}, u32[]{:S(2)}) %collective-permute-start) | collective-permute-done | bytes 49184 | tf_op jit(solution)/shard_map/ppermute | solution.py:234
  50.1 0.0 all-to-all-done.recv_ref
  50.1 0.6 copy-done.5
  50.7 0.7 copy-done.1
  51.3 19.3 %shard_map.105 = (f32[16,16,6,128]{3,2,1,0:T(8,128)}, f32[16,16,6,128]{3,2,1,0:T(8,128)}) custom-call(f32[16,16,6,128]{3,2,1,0:T(8,128)} %copy.13.adj_ref, f32[16,16,6,128]{3,2,1,0:T(8,128)} %copy.14.src_ref, f32[16,16,128]{2,1,0:T(8,128)} %step_ref.1, bf16[32,16,128]{2,1,0:T(8,128)(2,1)} %copy-done.1, f32[16,6,128]{2,1,0:T(8,128)} %copy-done.5, ...), custom_call_target="tpu_custom_call" | custom-call | tf_op jit(solution)/shard_map/pallas_call | solution.py:280
  70.7 2.2 %copy.16 = f32[16,16,6,128]{3,1,2,0:T(8,128)} copy(f32[16,16,6,128]{3,2,1,0:T(8,128)} %get-tuple-element.6) | data formatting | bytes 1572864 | tf_op jit(solution)/shard_map/pallas_call | solution.py:280
  72.9 2.2 %copy.17 = f32[16,16,6,128]{3,1,2,0:T(8,128)} copy(f32[16,16,6,128]{3,2,1,0:T(8,128)} %get-tuple-element.7) | data formatting | bytes 1572864 | tf_op jit(solution)/shard_map/pallas_call | solution.py:280
  (9 shorter events, 0.0 us)
Async XLA Ops:
  1.3 19.4 %copy-start.6 = (f32[1024,3]{0,1:T(4,128)S(1)}, f32[1024,3]{0,1:T(4,128)}, u32[]{:S(2)}) copy-start(f32[1024,3]{0,1:T(4,128)} %param.17) | copy-start | bytes 36868
  20.6 26.3 %copy-start = (f32[16,16,6,128]{3,1,2,0:T(8,128)S(1)}, f32[16,16,6,128]{3,1,2,0:T(8,128)}, u32[]{:S(2)}) copy-start(f32[16,16,6,128]{3,1,2,0:T(8,128)} %param.11) | copy-start | bytes 2359300
  28.7 21.3 %all-to-all-start = ((bf16[32,16,128]{2,1,0:T(8,128)(2,1)}), bf16[32,16,128]{2,1,0:T(8,128)(2,1)S(1)}, u32[]{:S(2)}, u32[]{:S(2)}) async-start(bf16[32,16,128]{2,1,0:T(8,128)(2,1)} %get-tuple-element.4), calls=%async_computation | async-start | bytes 262144 | tf_op jit(solution)/shard_map/all_to_all | solution.py:274
  35.8 12.3 %collective-permute-start.3 = (f32[16,6,128]{2,1,0:T(8,128)S(1)}, f32[16,6,128]{2,1,0:T(8,128)S(1)}, u32[]{:S(2)}, u32[]{:S(2)}) collective-permute-start(f32[16,6,128]{2,1,0:T(8,128)S(1)} %get-tuple-element.8), channel_id=1, source_target_pairs={{1,0},{2,1},{3,2},{4,3},{5,4},{6,5},{7,6},{9,8},{10,9},{11,10},{12... | collective-permute-start | bytes 147464 | tf_op jit(solution)/shard_map/ppermute | solution.py:234
  38.3 9.9 %collective-permute-start.2 = (f32[16,6,128]{2,1,0:T(8,128)S(1)}, f32[16,6,128]{2,1,0:T(8,128)S(1)}, u32[]{:S(2)}, u32[]{:S(2)}) collective-permute-start(f32[16,6,128]{2,1,0:T(8,128)S(1)} %get-tuple-element.9), channel_id=1, source_target_pairs={{0,1},{1,2},{2,3},{3,4},{4,5},{5,6},{6,7},{8,9},{9,10},{10,11},{11... | collective-permute-start | bytes 147464 | tf_op jit(solution)/shard_map/ppermute | solution.py:234
  42.6 5.6 %collective-permute-start.1 = (f32[16,6,128]{2,1,0:T(8,128)S(1)}, f32[16,6,128]{2,1,0:T(8,128)S(1)}, u32[]{:S(2)}, u32[]{:S(2)}) collective-permute-start(f32[16,6,128]{2,1,0:T(8,128)S(1)} %get-tuple-element.10), channel_id=1, source_target_pairs={{8,0},{16,8},{24,16},{9,1},{17,9},{25,17},{10,2},{18,10},{26,18},{... | collective-permute-start | bytes 147464 | tf_op jit(solution)/shard_map/ppermute | solution.py:234
  44.5 5.6 %collective-permute-start = (f32[16,6,128]{2,1,0:T(8,128)S(1)}, f32[16,6,128]{2,1,0:T(8,128)S(1)}, u32[]{:S(2)}, u32[]{:S(2)}) collective-permute-start(f32[16,6,128]{2,1,0:T(8,128)S(1)} %get-tuple-element.11), channel_id=1, source_target_pairs={{0,8},{8,16},{16,24},{1,9},{9,17},{17,25},{2,10},{10,18},{18,26},{... | collective-permute-start | bytes 147464 | tf_op jit(solution)/shard_map/ppermute | solution.py:234
  48.1 1.9 %copy-start.2 = (f32[16,6,128]{2,1,0:T(8,128)}, f32[16,6,128]{2,1,0:T(8,128)S(1)}, u32[]{:S(2)}) copy-start(f32[16,6,128]{2,1,0:T(8,128)S(1)} %collective-permute-done.3.rim_yh) | copy-start | bytes 147460
  48.1 1.9 %copy-start.3 = (f32[16,6,128]{2,1,0:T(8,128)}, f32[16,6,128]{2,1,0:T(8,128)S(1)}, u32[]{:S(2)}) copy-start(f32[16,6,128]{2,1,0:T(8,128)S(1)} %collective-permute-done.2.rim_yl) | copy-start | bytes 147460
  48.2 1.9 %copy-start.4 = (f32[16,6,128]{2,1,0:T(8,128)}, f32[16,6,128]{2,1,0:T(8,128)S(1)}, u32[]{:S(2)}) copy-start(f32[16,6,128]{2,1,0:T(8,128)S(1)} %collective-permute-done.1.rim_xh) | copy-start | bytes 147460
  50.1 0.6 copy-start.5
  50.7 0.7 copy-start.1

commit v2 on v1

v2 whole, which is shorter than its diff:
```python
import functools

import jax
import jax.numpy as jnp
from jax import lax
from jax.experimental import pallas as pl
from jax.experimental.pallas import tpu as pltpu
from jax.sharding import PartitionSpec as P

F32 = jnp.float32
BF16 = jnp.bfloat16
VMEM_LIMIT = 56 * 1024 * 1024
NT = (((1,), (1,)), ((), ()))
MESH = pl.DeviceIdType.MESH
LANES = 128


def contracted(blocks, values, b):
    var_count = len(values)
    total = blocks(b).astype(F32) * values[0]
    for a in range(1, var_count):
        total += blocks(a * var_count + b).astype(F32) * values[a]
    return total


def low_of(adj_ref, x):
    return [adj_ref[x, a].astype(BF16).astype(F32) for a in range(adj_ref.shape[1])]


def pack_rows(count_ref, cell_ref, owner_ref, base_ref, frac_ref, adj_ref, masked_ref, picked_ref, me, blocks, stride):
    size_x, var_count, size_y, size_z = adj_ref.shape
    rows = cell_ref.shape[1]
    z_bits = size_z.bit_length() - 1
    row = lax.broadcasted_iota(jnp.int32, (1, rows), 1)
    live = row < count_ref[0]
    cell = cell_ref[...]
    cell_z = cell & (size_z - 1)
    cell_xy = cell >> z_bits
    hot_z = jnp.where(lax.broadcasted_iota(jnp.int32, (size_z, rows), 0) == cell_z, 1.0, 0.0).astype(BF16)
    picked_ref[...] = jnp.zeros(picked_ref.shape, F32)
    y_of = lax.broadcasted_iota(jnp.int32, (size_y, rows), 0)

    def gather(x, carry):
        plane = adj_ref[x].reshape(var_count * size_y, size_z).astype(BF16)
        found = jnp.dot(plane, hot_z, preferred_element_type=F32)
        here = y_of == cell_xy - x * size_y
        for a in range(var_count):
            at = slice(a * size_y, (a + 1) * size_y)
            picked_ref[at, :] = jnp.where(here, found[at], picked_ref[at, :])
        return carry

    lax.fori_loop(0, size_x, gather, 0)
    base = base_ref[...]
    base_xy = (base >> z_bits).astype(F32)
    base_z = (base & (size_z - 1)).astype(F32)
    sub = lax.broadcasted_iota(jnp.int32, (8, rows), 0)
    top = jnp.where(sub == var_count, base_xy, base_z)
    for a in range(var_count):
        mu = jnp.sum(picked_ref[a * size_y : (a + 1) * size_y, :], axis=0, keepdims=True)
        top = jnp.where(sub == a, mu, top)
    frac = frac_ref[...]
    frac_hi = frac.astype(BF16).astype(F32)
    payload = jnp.concatenate([top, frac_hi, frac - frac_hi], axis=0)
    owner = jnp.where(live, owner_ref[...], -1)

    strips = rows // LANES
    block_ids = lax.broadcasted_iota(jnp.int32, (blocks, LANES), 0)
    matches = [
        jnp.where(block_ids == owner[:, s * LANES : (s + 1) * LANES], 1.0, 0.0) for s in range(strips)
    ]
    first = lax.broadcasted_iota(jnp.int32, (LANES, LANES), 0)
    second = lax.broadcasted_iota(jnp.int32, (LANES, LANES), 1)
    before = jnp.where(first < second, 1.0, 0.0).astype(BF16)
    earlier = jnp.dot(jnp.concatenate(matches, axis=0).astype(BF16), before, preferred_element_type=F32)
    carry = jnp.zeros((blocks, 1), F32)
    ranks = []
    for s in range(strips):
        here = earlier[s * blocks : (s + 1) * blocks] + carry
        ranks.append(jnp.sum(here * matches[s], axis=0, keepdims=True))
        carry = carry + jnp.sum(matches[s], axis=1, keepdims=True)
    rank = jnp.concatenate(ranks, axis=1).astype(jnp.int32)
    place = rank + lax.rem(me, LANES // stride) * stride
    hot_rank = jnp.where(lax.broadcasted_iota(jnp.int32, (LANES, rows), 0) == place, 1.0, 0.0).astype(BF16)

    def mask(o, carry):
        masked_ref[pl.ds(pl.multiple_of(o * 16, 16), 16), :] = jnp.where(owner == o, payload, 0.0).astype(BF16)
        return carry

    lax.fori_loop(0, blocks, mask, 0)
    return lax.dot_general(masked_ref[...], hot_rank, NT, preferred_element_type=F32).astype(BF16)


def start_side(jac_hbm, side_ref, edge_ref, sems):
    size_x = jac_hbm.shape[0]
    copies = [
        pltpu.make_async_copy(jac_hbm.at[size_x - 1, 1], edge_ref.at[0], sems.at[0]),
        pltpu.make_async_copy(jac_hbm.at[0, 2], edge_ref.at[1], sems.at[1]),
        pltpu.make_async_copy(jac_hbm.at[:, pl.ds(3, 2)], side_ref, sems.at[2]),
    ]
    for copy in copies:
        copy.start()
    return copies


def side_flux(copies, adj_ref, side_ref, edge_ref, rimx_ref, rimy_ref, part_ref):
    size_x, var_count, size_y, size_z = adj_ref.shape
    for copy in copies:
        copy.wait()
    for i, x in enumerate((size_x - 1, 0)):
        low = low_of(adj_ref, x)
        for b in range(var_count):
            rimx_ref[i, b] = contracted(lambda n: edge_ref[i, n], low, b)
    y_of = lax.broadcasted_iota(jnp.int32, (size_y, size_z), 0)

    def plane(x, carry):
        low = low_of(adj_ref, x)
        for b in range(var_count):
            up = pltpu.roll(contracted(lambda n: side_ref[x, 0, n], low, b), 1, 0)
            down = pltpu.roll(contracted(lambda n: side_ref[x, 1, n], low, b), size_y - 1, 0)
            rimy_ref[0, x, b : b + 1, :] = up[0:1]
            rimy_ref[1, x, b : b + 1, :] = down[size_y - 1 : size_y]
            part_ref[x, b] = jnp.where(y_of == 0, 0.0, up) + jnp.where(y_of == size_y - 1, 0.0, down)
        return carry

    lax.fori_loop(0, size_x, plane, 0)


def plane_copies(jac_hbm, jac_ref, sems, x):
    return (
        pltpu.make_async_copy(jac_hbm.at[x, pl.ds(0, 3)], jac_ref.at[x, pl.ds(0, 3)], sems.at[x, 0]),
        pltpu.make_async_copy(jac_hbm.at[x, pl.ds(5, 2)], jac_ref.at[x, pl.ds(3, 2)], sems.at[x, 1]),
    )


def start_planes(jac_hbm, jac_ref, sems):
    def start(x, carry):
        for copy in plane_copies(jac_hbm, jac_ref, sems, x):
            copy.start()
        return carry

    lax.fori_loop(0, jac_hbm.shape[0], start, 0)


def main_flux(adj_ref, jac_hbm, jac_ref, low_ref, part_ref, flux_ref, sems):
    size_x, var_count, size_y, size_z = adj_ref.shape
    low_ref[0] = jnp.zeros(low_ref.shape[1:], F32)
    low_ref[size_x + 1] = jnp.zeros(low_ref.shape[1:], F32)

    def narrow(x, carry):
        low_ref[x + 1] = adj_ref[x].astype(BF16).astype(F32)
        return carry

    lax.fori_loop(0, size_x, narrow, 0)
    lane = lax.broadcasted_iota(jnp.int32, (size_y, size_z), 1)

    def wait(x):
        for copy in plane_copies(jac_hbm, jac_ref, sems, x):
            copy.wait()

    wait(0)

    def plane(x, carry):
        @pl.when(x + 1 < size_x)
        def _():
            wait(x + 1)

        lower = jnp.maximum(x - 1, 0)
        upper = jnp.minimum(x + 1, size_x - 1)
        mine = [low_ref[x + 1, a] for a in range(var_count)]
        below = [low_ref[x, a] for a in range(var_count)]
        above = [low_ref[x + 2, a] for a in range(var_count)]
        for b in range(var_count):
            up = pltpu.roll(contracted(lambda n: jac_ref[x, 3, n], mine, b), 1, 1)
            down = pltpu.roll(contracted(lambda n: jac_ref[x, 4, n], mine, b), size_z - 1, 1)
            total = part_ref[x, b] + contracted(lambda n: jac_ref[x, 0, n], mine, b)
            total += contracted(lambda n: jac_ref[lower, 1, n], below, b)
            total += contracted(lambda n: jac_ref[upper, 2, n], above, b)
            total += jnp.where(lane == 0, 0.0, up) + jnp.where(lane == size_z - 1, 0.0, down)
            flux_ref[x, b] = total
        return carry

    lax.fori_loop(0, size_x, plane, 0)


class Exchange:
    def __init__(self, near_count, off_count, tiles_ref, rimx_ref, rimy_ref, recv_ref, gotx_ref, goty_ref, sems):
        self.near_count, self.off_count = near_count, off_count
        self.blocks = near_count * off_count
        self.near, self.off = lax.axis_index("near"), lax.axis_index("off")
        self.me = self.near * off_count + self.off
        self.tiles, self.rimx, self.rimy = tiles_ref, rimx_ref, rimy_ref
        self.recv, self.gotx, self.goty = recv_ref, gotx_ref, goty_ref
        self.tile_send, self.tile_recv, self.rim_send, self.rim_recv, self.own = sems

    def device(self, block):
        return (block // self.off_count, lax.rem(block, self.off_count))

    def announce(self):
        barrier = pltpu.get_barrier_semaphore()

        def greet(d, carry):
            other = lax.rem(self.me + d, self.blocks)
            pl.semaphore_signal(barrier, inc=1, device_id=self.device(other), device_id_type=MESH)
            return carry

        lax.fori_loop(1, self.blocks, greet, 0)

    def meet(self):
        pl.semaphore_wait(pltpu.get_barrier_semaphore(), self.blocks - 1)

    def tile(self, d, block, slot):
        return pltpu.make_async_remote_copy(
            src_ref=self.tiles.at[block],
            dst_ref=self.recv.at[slot],
            send_sem=self.tile_send.at[d],
            recv_sem=self.tile_recv.at[d],
            device_id=self.device(block),
            device_id_type=MESH,
        )

    def own_tile(self):
        return pltpu.make_async_copy(self.tiles.at[self.me], self.recv.at[self.me], self.own)

    def rims(self):
        routes = (
            (self.rimx, self.gotx, 0, (self.near + 1, self.off), self.near < self.near_count - 1, self.near > 0),
            (self.rimx, self.gotx, 1, (self.near - 1, self.off), self.near > 0, self.near < self.near_count - 1),
            (self.rimy, self.goty, 0, (self.near, self.off + 1), self.off < self.off_count - 1, self.off > 0),
            (self.rimy, self.goty, 1, (self.near, self.off - 1), self.off > 0, self.off < self.off_count - 1),
        )
        return [
            (
                pltpu.make_async_remote_copy(
                    src_ref=source.at[i],
                    dst_ref=target.at[i],
                    send_sem=self.rim_send.at[n],
                    recv_sem=self.rim_recv.at[n],
                    device_id=device,
                    device_id_type=MESH,
                ),
                sends,
                gets,
            )
            for n, (source, target, i, device, sends, gets) in enumerate(routes)
        ]

    def send_tiles(self):
        def send(d, carry):
            self.tile(d, lax.rem(self.me + d, self.blocks), self.me).start()
            return carry

        self.own_tile().start()
        lax.fori_loop(1, self.blocks, send, 0)

    def send_rims(self):
        for copy, sends, _ in self.rims():
            pl.when(sends)(copy.start)

    def finish(self):
        def end(d, carry):
            self.tile(d, lax.rem(self.me + d, self.blocks), self.me).wait_send()
            sender = lax.rem(self.me + self.blocks - d, self.blocks)
            self.tile(d, sender, sender).wait_recv()
            return carry

        self.own_tile().wait()
        lax.fori_loop(1, self.blocks, end, 0)
        for copy, sends, gets in self.rims():
            pl.when(sends)(copy.wait_send)
            pl.when(gets)(copy.wait_recv)


def add_rims(exchange, gotx_ref, goty_ref, flux_ref):
    size_x, var_count, size_y, size_z = flux_ref.shape

    @pl.when(exchange.near > 0)
    def _():
        flux_ref[0] += gotx_ref[0]

    @pl.when(exchange.near < exchange.near_count - 1)
    def _():
        flux_ref[size_x - 1] += gotx_ref[1]

    def add(i, y):
        def plane(x, carry):
            rows = goty_ref[i, x]
            for b in range(var_count):
                flux_ref[x, b, y : y + 1, :] += rows[b : b + 1]
            return carry

        lax.fori_loop(0, size_x, plane, 0)

    @pl.when(exchange.off > 0)
    def _():
        add(0, 0)

    @pl.when(exchange.off < exchange.off_count - 1)
    def _():
        add(1, size_y - 1)


def exchange_kernel(near_count, off_count, stride, count_ref, cell_ref, owner_ref, base_ref, frac_ref, adj_ref, jac_hbm,
                    flux_ref, recv_out, side_ref, edge_ref, masked_ref, picked_ref, tiles_ref, rimx_ref, rimy_ref,
                    part_ref, jac_ref, low_ref, recv_ref, gotx_ref, goty_ref, side_sems, plane_sems, *sems):
    exchange = Exchange(near_count, off_count, tiles_ref, rimx_ref, rimy_ref, recv_ref, gotx_ref, goty_ref, sems)
    exchange.announce()
    copies = start_side(jac_hbm, side_ref, edge_ref, side_sems)
    start_planes(jac_hbm, jac_ref, plane_sems)
    tiles = pack_rows(count_ref, cell_ref, owner_ref, base_ref, frac_ref, adj_ref, masked_ref, picked_ref,
                      exchange.me, exchange.blocks, stride)
    tiles_ref[...] = tiles.reshape(exchange.blocks, 16, LANES)
    exchange.meet()
    exchange.send_tiles()
    side_flux(copies, adj_ref, side_ref, edge_ref, rimx_ref, rimy_ref, part_ref)
    exchange.send_rims()
    main_flux(adj_ref, jac_hbm, jac_ref, low_ref, part_ref, flux_ref, plane_sems)
    exchange.finish()
    add_rims(exchange, gotx_ref, goty_ref, flux_ref)
    recv_out[...] = recv_ref[...]


def overset_factors(recv_ref, stride, size_x, size_y, size_z, var_count):
    blocks = recv_ref.shape[0]
    group = LANES // stride
    mus, wxs, wys, wzs = [], [], [], []
    y_bits = size_y.bit_length() - 1

    def hat(index, fraction, length):
        at = lax.broadcasted_iota(jnp.int32, (length, LANES), 0)
        return jnp.where(at == index, 1.0 - fraction, jnp.where(at == index + 1, fraction, 0.0))

    for g in range(blocks // group):
        tile = recv_ref[g * group].astype(F32)
        for i in range(1, group):
            tile = tile + recv_ref[g * group + i].astype(F32)
        frac = tile[8:12] + tile[12:16]
        xy = tile[var_count : var_count + 1].astype(jnp.int32)
        z = tile[var_count + 1 : var_count + 2].astype(jnp.int32)
        mus.append(-tile[0:8])
        wxs.append(hat(xy >> y_bits, frac[0:1], size_x))
        wys.append(hat(xy & (size_y - 1), frac[1:2], size_y))
        wzs.append(hat(z, frac[2:3], size_z))
    return tuple(jnp.concatenate(part, axis=1) for part in (mus, wxs, wys, wzs))


def finish_kernel(stride, size_x, adj_ref, src_ref, step_ref, flux_ref, recv_ref, res_ref, upd_ref,
                  mu_ref, wx_ref, wy_ref, wz_ref, left_ref):
    planes, var_count, size_y, size_z = adj_ref.shape
    chunk = pl.program_id(0)

    @pl.when(chunk == 0)
    def _():
        mu, wx, wy, wz = overset_factors(recv_ref, stride, size_x, size_y, size_z, var_count)
        mu_ref[...] = mu
        wx_ref[...] = wx
        wy_ref[...] = wy
        wz_hi = wz.astype(BF16)
        wz_ref[0] = wz_hi
        wz_ref[1] = (wz - wz_hi.astype(F32)).astype(BF16)

    for p in range(planes):
        wxy = wy_ref[...] * wx_ref[pl.ds(chunk * planes + p, 1), :]
        for b in range(var_count):
            at = (p * var_count + b) * size_y
            left_ref[at : at + size_y, :] = (wxy * mu_ref[b : b + 1, :]).astype(BF16)
    left = left_ref[...]
    over = lax.dot_general(left, wz_ref[0], NT, preferred_element_type=F32)
    over += lax.dot_general(left, wz_ref[1], NT, preferred_element_type=F32)
    res = flux_ref[...] + over.reshape(planes, var_count, size_y, size_z) + src_ref[...]
    res_ref[...] = res
    upd_ref[...] = adj_ref[...] - step_ref[...][:, None] * res


def shards(adjoint, jacobian, source, pseudo_step, receptor_count, receptor_cell, donor_owner, donor_base, donor_fraction):
    size_x, size_y, var_count, size_z = adjoint.shape
    rows = var_count * var_count
    near_count, off_count = lax.axis_size("near"), lax.axis_size("off")
    blocks = near_count * off_count
    row_count = receptor_cell.shape[0]
    capacity = max(2, 3 * row_count // (2 * blocks))
    stride = 1 << (capacity - 1).bit_length()
    slots = blocks * stride
    vmem = pl.BlockSpec(memory_space=pltpu.VMEM)
    smem = pl.BlockSpec(memory_space=pltpu.SMEM)
    hbm = pl.BlockSpec(memory_space=pl.ANY)
    adj = jnp.transpose(adjoint, (0, 2, 1, 3))
    src = jnp.transpose(source, (0, 2, 1, 3))
    jac = jnp.transpose(jacobian, (0, 2, 3, 1, 4))
    frac = jnp.pad(donor_fraction.T, ((0, 1), (0, 0)))
    receptors = (
        receptor_count,
        receptor_cell.reshape(1, row_count),
        donor_owner.reshape(1, row_count),
        donor_base.reshape(1, row_count),
        frac,
    )
    tiles_shape = (blocks, 16, LANES)
    rimx_shape = (2, var_count, size_y, size_z)
    rimy_shape = (2, size_x, var_count, size_z)
    side_scratch = [
        pltpu.VMEM((size_x, 2, rows, size_y, size_z), BF16),
        pltpu.VMEM((2, rows, size_y, size_z), BF16),
        pltpu.VMEM((blocks * 16, row_count), BF16),
        pltpu.VMEM((var_count * size_y, row_count), F32),
    ]
    exchange_scratch = [
        pltpu.VMEM((size_x, 5, rows, size_y, size_z), BF16),
        pltpu.VMEM((size_x + 2, var_count, size_y, size_z), F32),
        pltpu.VMEM(tiles_shape, BF16),
        pltpu.VMEM(rimx_shape, F32),
        pltpu.VMEM(rimy_shape, F32),
    ]
    exchange_sems = [
        pltpu.SemaphoreType.DMA((size_x, 2)),
        pltpu.SemaphoreType.DMA((blocks,)),
        pltpu.SemaphoreType.DMA((blocks,)),
        pltpu.SemaphoreType.DMA((4,)),
        pltpu.SemaphoreType.DMA((4,)),
        pltpu.SemaphoreType.DMA,
    ]
    exchange_out = (jax.ShapeDtypeStruct(adj.shape, F32), jax.ShapeDtypeStruct(tiles_shape, BF16))
    flux, received = pl.pallas_call(
        functools.partial(exchange_kernel, near_count, off_count, stride),
        out_shape=exchange_out,
        in_specs=[smem] + [vmem] * 5 + [hbm],
        out_specs=(vmem, vmem),
        scratch_shapes=side_scratch
        + [
            pltpu.VMEM(tiles_shape, BF16),
            pltpu.VMEM(rimx_shape, F32),
            pltpu.VMEM(rimy_shape, F32),
            pltpu.VMEM(adj.shape, F32),
        ]
        + exchange_scratch
        + [pltpu.SemaphoreType.DMA((3,))]
        + exchange_sems,
        compiler_params=pltpu.CompilerParams(vmem_limit_bytes=VMEM_LIMIT, collective_id=0, has_side_effects=True),
    )(*receptors, adj, jac)
    planes = 4 if size_x % 4 == 0 else 1
    field = pl.BlockSpec((planes, var_count, size_y, size_z), lambda i: (i, 0, 0, 0))
    residual, updated = pl.pallas_call(
        functools.partial(finish_kernel, stride, size_x),
        grid=(size_x // planes,),
        out_shape=(jax.ShapeDtypeStruct(adj.shape, F32), jax.ShapeDtypeStruct(adj.shape, F32)),
        in_specs=[
            field,
            field,
            pl.BlockSpec((planes, size_y, size_z), lambda i: (i, 0, 0)),
            field,
            pl.BlockSpec(tiles_shape, lambda i: (0, 0, 0)),
        ],
        out_specs=(field, field),
        scratch_shapes=[
            pltpu.VMEM((8, slots), F32),
            pltpu.VMEM((size_x, slots), F32),
            pltpu.VMEM((size_y, slots), F32),
            pltpu.VMEM((2, size_z, slots), BF16),
            pltpu.VMEM((planes * var_count * size_y, slots), BF16),
        ],
        compiler_params=pltpu.CompilerParams(vmem_limit_bytes=VMEM_LIMIT),
    )(adj, src, pseudo_step, flux, received)
    return jnp.transpose(residual, (0, 2, 1, 3)), jnp.transpose(updated, (0, 2, 1, 3))


def solution(mesh):
    in_specs = (
        P("near", "off", None, None),
        P("near", "off", None, None, None),
        P("near", "off", None, None),
        P("near", "off", None),
        P(("near", "off")),
        P(("near", "off")),
        P(("near", "off"), None),
        P(("near", "off")),
        P(("near", "off"), None),
    )
    out_specs = (P("near", "off", None, None), P("near", "off", None, None))
    return jax.shard_map(shards, mesh=mesh, in_specs=in_specs, out_specs=out_specs, check_vma=False)
```

time: 75.7 us -> 26.8 us (0.35)
  the two profiles are of different devices: /device:TPU:6 before, /device:TPU:0 now
where the time goes in v2:
time: 26.8 us; the launch traced here: 26.6 us
  Pallas kernels  24 us (90%)
  local copies, waits for them, and re-layouts  1.33 us (5%)
  between operations  1.28 us (5%)
    pallas_call x1, Pallas kernels, shards(): pl.pallas_call(functools.partial(exchange_kernel, near_count, off_count,...  17.2 us
    pallas_call x1, Pallas kernels, shards(): pl.pallas_call(functools.partial(finish_kernel, stride, size_x), grid=(si...  6.78 us
    pad x1, local copies, waits for them, and re-layouts, shards(): frac = jnp.pad(donor_fraction.T, ((0, 1), (0, 0)))  1.33 us

profile of v2, /device:TPU:0, one launch (start us, length us, event | category | flops | bytes accessed | tf_op | source)
XLA Modules:
  0.0 26.6 jit_solution(3165217750043360248)
XLA Ops:
  1.3 1.3 %pad.4.frac_ref = f32[4,1024]{1,0:T(4,128)} pad(f32[3,1024]{1,0:T(4,128)} %bitcast.13, f32[]{:T(128)} %constant.2.clone.1), padding=0_1x0_0 | pad | bytes 28676 | tf_op jit(solution)/shard_map/jit(_pad)/pad | solution.py:389
  2.6 17.2 %shard_map.104 = (f32[16,6,16,128]{3,2,1,0:T(8,128)}, bf16[32,16,128]{2,1,0:T(8,128)(2,1)}) custom-call(s32[1]{0:T(128)S(6)} %copy.11.count_ref, s32[1,1024]{1,0:T(1,128)} %bitcast.14, s32[1,1024]{1,0:T(1,128)} %bitcast.15, s32[1,1024]{1,0:T(1,128)} %bitcast.16, f32[4,1024]{1,0:T(4,128)} %pad.4.frac_ref, f32[16,6,16,128]{3,2,1,0:T(8,128)} %bitcast.10, ...), custom_call_target="tpu_custom_call" | custom-call | tf_op jit(solution)/shard_map/pallas_call | solution.py:422
  19.8 6.8 %shard_map.105 = (f32[16,6,16,128]{3,2,1,0:T(8,128)}, f32[16,6,16,128]{3,2,1,0:T(8,128)}) custom-call(f32[16,6,16,128]{3,2,1,0:T(8,128)} %bitcast.11, f32[16,6,16,128]{3,2,1,0:T(8,128)} %bitcast.12, f32[16,16,128]{2,1,0:T(8,128)} %step_ref.1, f32[16,6,16,128]{3,2,1,0:T(8,128)} %get-tuple-element.6.flux_ref, bf16[32,16,128]{2,1,0:T(8,128)(2,1)} %get-tuple-element.7.recv_ref), custom_call_target="tpu_custom_call" | custom-call | tf_op jit(solution)/shard_map/pallas_call | solution.py:441

commit v3 on v2

--- a/solution.py
+++ b/solution.py
@@ -40,16 +40,24 @@
     picked_ref[...] = jnp.zeros(picked_ref.shape, F32)
     y_of = lax.broadcasted_iota(jnp.int32, (size_y, rows), 0)
 
-    def gather(x, carry):
-        plane = adj_ref[x].reshape(var_count * size_y, size_z).astype(BF16)
+    planes = 4 if size_x % 4 == 0 else 1
+    height = var_count * size_y
+
+    def gather(step, carry):
+        first_x = step * planes
+        plane = adj_ref[pl.ds(first_x, planes)].reshape(planes * height, size_z).astype(BF16)
         found = jnp.dot(plane, hot_z, preferred_element_type=F32)
-        here = y_of == cell_xy - x * size_y
+        here = [y_of == cell_xy - (first_x + p) * size_y for p in range(planes)]
         for a in range(var_count):
             at = slice(a * size_y, (a + 1) * size_y)
-            picked_ref[at, :] = jnp.where(here, found[at], picked_ref[at, :])
-        return carry
-
-    lax.fori_loop(0, size_x, gather, 0)
+            chosen = picked_ref[at, :]
+            for p in range(planes):
+                start = p * height + a * size_y
+                chosen = jnp.where(here[p], found[start : start + size_y], chosen)
+            picked_ref[at, :] = chosen
+        return carry
+
+    lax.fori_loop(0, size_x // planes, gather, 0)
     base = base_ref[...]
     base_xy = (base >> z_bits).astype(F32)
     base_z = (base & (size_z - 1)).astype(F32)
@@ -58,9 +66,10 @@
     for a in range(var_count):
         mu = jnp.sum(picked_ref[a * size_y : (a + 1) * size_y, :], axis=0, keepdims=True)
         top = jnp.where(sub == a, mu, top)
-    frac = frac_ref[...]
+    axis = sub & 3
+    frac = jnp.where(axis == 0, frac_ref[0:1, :], jnp.where(axis == 1, frac_ref[1:2, :], frac_ref[2:3, :]))
     frac_hi = frac.astype(BF16).astype(F32)
-    payload = jnp.concatenate([top, frac_hi, frac - frac_hi], axis=0)
+    payload = jnp.concatenate([top, jnp.where(sub < 4, frac_hi, frac - frac_hi)], axis=0)
     owner = jnp.where(live, owner_ref[...], -1)
 
     strips = rows // LANES
@@ -344,7 +353,7 @@
 
 
 def finish_kernel(stride, size_x, adj_ref, src_ref, step_ref, flux_ref, recv_ref, res_ref, upd_ref,
-                  mu_ref, wx_ref, wy_ref, wz_ref, left_ref):
+                  mu_ref, wx_ref, wy_ref, wz_ref):
     planes, var_count, size_y, size_z = adj_ref.shape
     chunk = pl.program_id(0)
 
@@ -355,17 +364,20 @@
         wx_ref[...] = wx
         wy_ref[...] = wy
         wz_hi = wz.astype(BF16)
-        wz_ref[0] = wz_hi
-        wz_ref[1] = (wz - wz_hi.astype(F32)).astype(BF16)
-
-    for p in range(planes):
-        wxy = wy_ref[...] * wx_ref[pl.ds(chunk * planes + p, 1), :]
-        for b in range(var_count):
-            at = (p * var_count + b) * size_y
-            left_ref[at : at + size_y, :] = (wxy * mu_ref[b : b + 1, :]).astype(BF16)
-    left = left_ref[...]
-    over = lax.dot_general(left, wz_ref[0], NT, preferred_element_type=F32)
-    over += lax.dot_general(left, wz_ref[1], NT, preferred_element_type=F32)
+        wz_ref[0:size_z, :] = wz_hi
+        wz_ref[size_z : 2 * size_z, :] = (wz - wz_hi.astype(F32)).astype(BF16)
+
+    slots = wz_ref.shape[1]
+    width = min(slots, 2 * LANES)
+    both = jnp.zeros((planes * var_count * size_y, 2 * size_z), F32)
+    for k in range(0, slots, width):
+        at = slice(k, k + width)
+        left = []
+        for p in range(planes):
+            wxy = wy_ref[:, at] * wx_ref[pl.ds(chunk * planes + p, 1), at]
+            left += [(wxy * mu_ref[b : b + 1, at]).astype(BF16) for b in range(var_count)]
+        both += lax.dot_general(jnp.concatenate(left, axis=0), wz_ref[:, at], NT, preferred_element_type=F32)
+    over = both[:, 0:size_z] + both[:, size_z : 2 * size_z]
     res = flux_ref[...] + over.reshape(planes, var_count, size_y, size_z) + src_ref[...]
     res_ref[...] = res
     upd_ref[...] = adj_ref[...] - step_ref[...][:, None] * res
@@ -386,13 +398,12 @@
     adj = jnp.transpose(adjoint, (0, 2, 1, 3))
     src = jnp.transpose(source, (0, 2, 1, 3))
     jac = jnp.transpose(jacobian, (0, 2, 3, 1, 4))
-    frac = jnp.pad(donor_fraction.T, ((0, 1), (0, 0)))
     receptors = (
         receptor_count,
         receptor_cell.reshape(1, row_count),
         donor_owner.reshape(1, row_count),
         donor_base.reshape(1, row_count),
-        frac,
+        donor_fraction.T,
     )
     tiles_shape = (blocks, 16, LANES)
     rimx_shape = (2, var_count, size_y, size_z)
@@ -454,8 +465,7 @@
             pltpu.VMEM((8, slots), F32),
             pltpu.VMEM((size_x, slots), F32),
             pltpu.VMEM((size_y, slots), F32),
-            pltpu.VMEM((2, size_z, slots), BF16),
-            pltpu.VMEM((planes * var_count * size_y, slots), BF16),
+            pltpu.VMEM((2 * size_z, slots), BF16),
         ],
         compiler_params=pltpu.CompilerParams(vmem_limit_bytes=VMEM_LIMIT),
     )(adj, src, pseudo_step, flux, received)

time: 26.8 us -> 22.6 us (0.84)
  Pallas kernels: 24 us -> 21.1 us
  local copies, waits for them, and re-layouts: 1.33 us -> 0 us
    pallas_call x1, Pallas kernels: 17.2 us -> 15.4 us  [shards(): pl.pallas_call(functools.partial(exchange_kernel, near_count, off_count,...]
    pad x1 -> x0, local copies, waits for them, and re-layouts: 1.33 us -> none  [shards(): frac = jnp.pad(donor_fraction.T, ((0, 1), (0, 0)))]
    pallas_call x1, Pallas kernels: 6.78 us -> 5.68 us  [shards(): pl.pallas_call(functools.partial(finish_kernel, stride, size_x), grid=(si...]
where the time goes in v3:
time: 22.6 us; the launch traced here: 22.4 us
  Pallas kernels  21.1 us (93%)
  between operations  1.28 us (6%)
    pallas_call x1, Pallas kernels, shards(): pl.pallas_call(functools.partial(exchange_kernel, near_count, off_count,...  15.4 us
    pallas_call x1, Pallas kernels, shards(): pl.pallas_call(functools.partial(finish_kernel, stride, size_x), grid=(si...  5.68 us

profile of v3, /device:TPU:0, one launch (start us, length us, event | category | flops | bytes accessed | tf_op | source)
XLA Modules:
  0.0 22.4 jit_solution(3228627607314034973)
XLA Ops:
  1.3 15.4 %shard_map.104 = (f32[16,6,16,128]{3,2,1,0:T(8,128)}, bf16[32,16,128]{2,1,0:T(8,128)(2,1)}) custom-call(s32[1]{0:T(128)S(6)} %copy.11.count_ref, s32[1,1024]{1,0:T(1,128)} %bitcast.14, s32[1,1024]{1,0:T(1,128)} %bitcast.15, s32[1,1024]{1,0:T(1,128)} %bitcast.16, f32[3,1024]{1,0:T(4,128)} %bitcast.13, f32[16,6,16,128]{3,2,1,0:T(8,128)} %bitcast.10, ...), custom_call_target="tpu_custom_call" | custom-call | tf_op jit(solution)/shard_map/pallas_call | solution.py:433
  16.7 5.7 %shard_map.105 = (f32[16,6,16,128]{3,2,1,0:T(8,128)}, f32[16,6,16,128]{3,2,1,0:T(8,128)}) custom-call(f32[16,6,16,128]{3,2,1,0:T(8,128)} %bitcast.11, f32[16,6,16,128]{3,2,1,0:T(8,128)} %bitcast.12, f32[16,16,128]{2,1,0:T(8,128)} %step_ref.1, f32[16,6,16,128]{3,2,1,0:T(8,128)} %get-tuple-element.6.flux_ref, bf16[32,16,128]{2,1,0:T(8,128)(2,1)} %get-tuple-element.7.recv_ref), custom_call_target="tpu_custom_call" | custom-call | tf_op jit(solution)/shard_map/pallas_call | solution.py:452

commit v4 on v3

--- a/solution.py
+++ b/solution.py
@@ -95,7 +95,7 @@
         masked_ref[pl.ds(pl.multiple_of(o * 16, 16), 16), :] = jnp.where(owner == o, payload, 0.0).astype(BF16)
         return carry
 
-    lax.fori_loop(0, blocks, mask, 0)
+    lax.fori_loop(0, blocks, mask, 0, unroll=4)
     return lax.dot_general(masked_ref[...], hot_rank, NT, preferred_element_type=F32).astype(BF16)
 
 
@@ -348,8 +348,8 @@
         mus.append(-tile[0:8])
         wxs.append(hat(xy >> y_bits, frac[0:1], size_x))
         wys.append(hat(xy & (size_y - 1), frac[1:2], size_y))
-        wzs.append(hat(z, frac[2:3], size_z))
-    return tuple(jnp.concatenate(part, axis=1) for part in (mus, wxs, wys, wzs))
+        wzs.append(hat(z, frac[2:3], size_z).T)
+    return tuple(jnp.concatenate(part, axis=1) for part in (mus, wxs, wys)) + (jnp.concatenate(wzs, axis=0),)
 
 
 def finish_kernel(stride, size_x, adj_ref, src_ref, step_ref, flux_ref, recv_ref, res_ref, upd_ref,
@@ -364,10 +364,10 @@
         wx_ref[...] = wx
         wy_ref[...] = wy
         wz_hi = wz.astype(BF16)
-        wz_ref[0:size_z, :] = wz_hi
-        wz_ref[size_z : 2 * size_z, :] = (wz - wz_hi.astype(F32)).astype(BF16)
-
-    slots = wz_ref.shape[1]
+        wz_ref[:, 0:size_z] = wz_hi
+        wz_ref[:, size_z : 2 * size_z] = (wz - wz_hi.astype(F32)).astype(BF16)
+
+    slots = wz_ref.shape[0]
     width = min(slots, 2 * LANES)
     both = jnp.zeros((planes * var_count * size_y, 2 * size_z), F32)
     for k in range(0, slots, width):
@@ -376,7 +376,7 @@
         for p in range(planes):
             wxy = wy_ref[:, at] * wx_ref[pl.ds(chunk * planes + p, 1), at]
             left += [(wxy * mu_ref[b : b + 1, at]).astype(BF16) for b in range(var_count)]
-        both += lax.dot_general(jnp.concatenate(left, axis=0), wz_ref[:, at], NT, preferred_element_type=F32)
+        both += jnp.dot(jnp.concatenate(left, axis=0), wz_ref[at, :], preferred_element_type=F32)
     over = both[:, 0:size_z] + both[:, size_z : 2 * size_z]
     res = flux_ref[...] + over.reshape(planes, var_count, size_y, size_z) + src_ref[...]
     res_ref[...] = res
@@ -465,7 +465,7 @@
             pltpu.VMEM((8, slots), F32),
             pltpu.VMEM((size_x, slots), F32),
             pltpu.VMEM((size_y, slots), F32),
-            pltpu.VMEM((2 * size_z, slots), BF16),
+            pltpu.VMEM((slots, 2 * size_z), BF16),
         ],
         compiler_params=pltpu.CompilerParams(vmem_limit_bytes=VMEM_LIMIT),
     )(adj, src, pseudo_step, flux, received)

time: 22.6 us -> 22.4 us (level)
  no operation moved by 1% of the time
where the time goes in v4:
time: 22.4 us; the launch traced here: 22.2 us
  Pallas kernels  20.9 us (93%)
  between operations  1.28 us (6%)
    pallas_call x1, Pallas kernels, shards(): pl.pallas_call(functools.partial(exchange_kernel, near_count, off_count,...  15.4 us
    pallas_call x1, Pallas kernels, shards(): pl.pallas_call(functools.partial(finish_kernel, stride, size_x), grid=(si...  5.54 us

profile of v4, /device:TPU:0, one launch (start us, length us, event | category | flops | bytes accessed | tf_op | source)
XLA Modules:
  0.0 22.2 jit_solution(14071035108573264347)
XLA Ops:
  1.3 15.4 %shard_map.104 = (f32[16,6,16,128]{3,2,1,0:T(8,128)}, bf16[32,16,128]{2,1,0:T(8,128)(2,1)}) custom-call(s32[1]{0:T(128)S(6)} %copy.11.count_ref, s32[1,1024]{1,0:T(1,128)} %bitcast.14, s32[1,1024]{1,0:T(1,128)} %bitcast.15, s32[1,1024]{1,0:T(1,128)} %bitcast.16, f32[3,1024]{1,0:T(4,128)} %bitcast.13, f32[16,6,16,128]{3,2,1,0:T(8,128)} %bitcast.10, ...), custom_call_target="tpu_custom_call" | custom-call | tf_op jit(solution)/shard_map/pallas_call | solution.py:433
  16.7 5.5 %shard_map.105 = (f32[16,6,16,128]{3,2,1,0:T(8,128)}, f32[16,6,16,128]{3,2,1,0:T(8,128)}) custom-call(f32[16,6,16,128]{3,2,1,0:T(8,128)} %bitcast.11, f32[16,6,16,128]{3,2,1,0:T(8,128)} %bitcast.12, f32[16,16,128]{2,1,0:T(8,128)} %step_ref.1, f32[16,6,16,128]{3,2,1,0:T(8,128)} %get-tuple-element.6.flux_ref, bf16[32,16,128]{2,1,0:T(8,128)(2,1)} %get-tuple-element.7.recv_ref), custom_call_target="tpu_custom_call" | custom-call | tf_op jit(solution)/shard_map/pallas_call | solution.py:452
